TPU v7x, 256 devices: a whole 4x4x8 slice. The times are simulated.
256 devices in a mesh: dp: 8 (over z), mp: 32 (over y, x, core).
Axes of the slice: x: 4, y: 4, z: 8, core: 2. Of those that a mesh axis runs over, the one named last changes fastest.
Arguments:
- hidden_acts: bfloat16 [5120, 28672], P('dp', 'mp'), may hold values from -6 to 6
- out_grads: bfloat16 [5120, 8192], P('dp', 'mp'), may hold values from -6 to 6
- query_in: bfloat16 [64, 32, 28672], P('dp', None, 'mp'), may hold values from -0.0625 to 0.0625
- query_out: bfloat16 [64, 32, 8192], P('dp', None, 'mp'), may hold values from -0.125 to 0.125
- seq_ids: int32 [8, 640], P('dp'), may hold values from 0 to 15, never falling along the last dimension, each value on 1 to 80 neighbouring positions
Outputs:
- scores: float32 [128, 64], P('dp', 'mp')
Inputs may be any that keep to these rules, and one draw needn't show every extreme that they name: `seq_ids`: in each row, ids never fall along the tokens, and every id of 0 to 15 covers 1 to 80 tokens, one exactly 80.
All inputs are finite; a program needn't handle non-finite values.
Results may differ from a plain program's by a relative error of at most 0.0003.
Values may be sent and summed in bfloat16 or wider, within the bound.
A program may use at most 64 MiB of HBM per device.

v0:
```python
import math

import jax
import jax.numpy as jnp
from jax import lax
from jax.sharding import PartitionSpec as P

R = 32
TOK_G = 640
SEQS = 16


def body(hidden_acts, out_grads, query_in, query_out, seq_ids):
    full_in, full_out = (
        lax.all_gather(query_in, "dp", axis=0, tiled=True),
        lax.all_gather(query_out, "dp", axis=0, tiled=True),
    )
    queries = full_in.shape[0]
    rank = full_in.shape[1]
    in_rows = full_in.reshape(queries * rank, full_in.shape[2])
    out_rows = full_out.reshape(queries * rank, full_out.shape[2])
    tokens = hidden_acts.shape[0]
    scale = 1.0 / math.sqrt(R * TOK_G / SEQS)
    labels = jnp.arange(SEQS, dtype=jnp.int32)
    contract = (((1,), (1,)), ((), ()))
    proj_in = lax.dot_general(in_rows, hidden_acts, contract, preferred_element_type=jnp.float32)
    proj_out = lax.dot_general(out_rows, out_grads, contract, preferred_element_type=jnp.float32)
    shares = lax.psum_scatter(
        jnp.stack([proj_in, proj_out], axis=1), "mp", scatter_dimension=0, tiled=True
    )
    local_q = shares.shape[0] // rank
    per_token = (shares[:, 0] * shares[:, 1]).reshape(local_q, rank, tokens).sum(axis=1)
    onehot = (seq_ids[0][None, :] == labels[:, None]).astype(jnp.float32)
    summed = lax.dot_general(onehot, per_token, contract, precision=lax.Precision.HIGHEST)
    return summed * scale


def solution(mesh):
    placed = (P("dp", "mp"), P("dp", "mp"), P("dp", None, "mp"), P("dp", None, "mp"), P("dp", None))
    return jax.shard_map(body, mesh=mesh, in_specs=placed, out_specs=P("dp", "mp"), check_vma=False)
```

profile of v0, /device:TPU:17, one launch (start us, length us, event | category | flops | bytes accessed | tf_op | source)
XLA Modules:
  0.0 222.3 jit_solution(7836054663614385743)
XLA Ops:
  6.5 0.0 copy-start
  6.5 0.0 all-gather.5.cloned.1.call-start
  6.5 0.7 all-gather.5.cloned.1.call-update
  7.3 0.0 all-gather.3.cloned.1.call-start
  7.3 0.7 all-gather.3.cloned.1.call-update
  8.0 0.0 reduce-scatter.2.cloned.1.call-start
  8.1 37.5 %all-gather.5.cloned.1.call-done = bf16[64,32,256]{2,1,0:T(8,128)(2,1)} async-done(((bf16[8,32,256]{2,1,0:T(8,128)(2,1)}), bf16[64,32,256]{2,1,0:T(8,128)(2,1)}) %all-gather.5.cloned.1.call-update) | async-done | bytes 1048592 | tf_op jit(solution)/shard_map/all_gather | solution.py:16
  45.6 4.6 %convolution_bitcast_fusion.1 = f32[2048,1,640]{2,0,1:T(8,128)} fusion(bf16[2048,256]{1,0:T(8,128)(2,1)} %bitcast.12, bf16[640,256]{1,0:T(8,128)(2,1)} %param.6), kind=kOutput, calls=%fused_computation.2 | convolution fusion | flops 671088640 | bytes 6619136 | tf_op jit(solution)/shard_map/dot_general | solution.py:27
  50.2 50.7 %all-gather.3.cloned.1.call-done = bf16[64,32,896]{2,1,0:T(8,128)(2,1)} async-done(((bf16[8,32,896]{2,1,0:T(8,128)(2,1)}), bf16[64,32,896]{2,1,0:T(8,128)(2,1)}) %all-gather.3.cloned.1.call-update) | async-done | bytes 3670032 | tf_op jit(solution)/shard_map/all_gather | solution.py:15
  100.9 0.0 copy-done
  100.9 0.0 copy-start.1
  100.9 5.5 %convolution_bitcast_fusion = f32[2048,1,640]{2,0,1:T(8,128)S(1)} fusion(bf16[2048,896]{1,0:T(8,128)(2,1)} %bitcast.14, bf16[640,896]{1,0:T(8,128)(2,1)S(1)} %copy-done), kind=kOutput, calls=%fused_computation.1 | convolution fusion | flops 2348810240 | bytes 10059776 | tf_op jit(solution)/shard_map/dot_general | solution.py:26
  106.4 0.0 copy-done.1
  106.4 4.6 %pad_maximum_fusion = f32[2048,2,640]{2,0,1:T(8,128)} fusion(f32[2048,1,640]{2,0,1:T(8,128)S(1)} %copy-done.1, f32[2048,1,640]{2,0,1:T(8,128)S(1)} %convolution_bitcast_fusion), kind=kLoop, calls=%fused_computation | loop fusion | flops 2621440 | bytes 20971520 | tf_op jit(solution)/shard_map/stack | solution.py:29
  111.1 0.0 copy-start.2
  111.1 0.0 reduce-scatter.2.cloned.1.call-update
  111.1 0.7 copy-done.2
  111.8 102.2 %reduce-scatter.2.cloned.1.call-done = f32[64,2,640]{2,0,1:T(8,128)} async-done(((f32[2048,2,640]{2,0,1:T(8,128)}), f32[64,2,640]{2,0,1:T(8,128)}) %reduce-scatter.2.cloned.1.call-update) | async-done | bytes 327696 | tf_op jit(solution)/shard_map/reduce_scatter | solution.py:28
  214.0 1.0 slice_multiply_fusion
  215.0 0.7 convolution_multiply_fusion
  (2 shorter events, 0.0 us)
Async XLA Ops:
  6.5 94.4 %copy-start = (bf16[640,896]{1,0:T(8,128)(2,1)S(1)}, bf16[640,896]{1,0:T(8,128)(2,1)}, u32[]{:S(2)}) copy-start(bf16[640,896]{1,0:T(8,128)(2,1)} %param.5) | copy-start | bytes 3440644
  6.5 39.1 %all-gather.5.cloned.1.call-start = ((), (), s32[]{:S(2)}) async-start(), calls=%async_computation.2 | async-start | bytes 1179648 | tf_op jit(solution)/shard_map/all_gather | solution.py:16
  7.3 93.6 %all-gather.3.cloned.1.call-start = ((), (), s32[]{:S(2)}) async-start(), calls=%async_computation.1 | async-start | bytes 4128768 | tf_op jit(solution)/shard_map/all_gather | solution.py:15
  8.0 206.0 %reduce-scatter.2.cloned.1.call-start = ((), (), s32[]{:S(2)}) async-start(), calls=%async_computation.3 | async-start | bytes 10813440 | tf_op jit(solution)/shard_map/reduce_scatter | solution.py:28
  100.9 5.5 %copy-start.1 = (f32[2048,1,640]{2,0,1:T(8,128)S(1)}, f32[2048,1,640]{2,0,1:T(8,128)}, u32[]{:S(2)}) copy-start(f32[2048,1,640]{2,0,1:T(8,128)} %convolution_bitcast_fusion.1) | copy-start | bytes 15728644
  111.1 0.7 copy-start.2
Sparse Core Ops, SparseCore 0:
  9.1 36.4 all-gather.4
  47.4 53.4 all-gather.2
  111.2 102.7 reduce-scatter.1
where the time goes:
time: 224 us; the launch traced here: 222 us
  waiting for transfers between devices  192 us (86%)
  between operations  13.1 us (6%)
  matrix products  10.8 us (5%)
  other arithmetic  5.7 us (3%)
    reduce_scatter x1, waiting for transfers between devices, body(): lax.psum_scatter(jnp.stack([proj_in, proj_out], axis=1), 'mp', scatter_di...  102 us
    all_gather x1, waiting for transfers between devices, body(): lax.all_gather(query_in, 'dp', axis=0, tiled=True)  50.7 us
    all_gather x1, waiting for transfers between devices, body(): lax.all_gather(query_out, 'dp', axis=0, tiled=True)  37.5 us
    dot_general x1, matrix products, body(): lax.dot_general(in_rows, hidden_acts, contract, preferred_element_type=jn...  5.52 us
    another operation x1, other arithmetic, body(): jnp.stack([proj_in, proj_out], axis=1)  4.64 us
    dot_general x1, matrix products, body(): lax.dot_general(out_rows, out_grads, contract, preferred_element_type=jnp...  4.6 us
  transfers between devices with their start and end apart: 3, of which 3 were waited for; matrix products, arithmetic and copies ran while one was open for 2% of the time, Pallas kernels for 0%

commit v1 on v0

v1 whole, which is shorter than its diff:
```python
import functools
import math

import jax
import jax.numpy as jnp
from jax import lax
from jax.experimental import pallas as pl
from jax.experimental.pallas import tpu as pltpu
from jax.sharding import PartitionSpec as P

R = 32
TOK = 640
SEQS = 16
NZ = 8
SIDE = 4
CHIPS = SIDE * SIDE
QH = 4
MESH = pl.DeviceIdType.MESH
NT = (((1,), (1,)), ((), ()))
SCALE = 1.0 / math.sqrt(R * TOK / SEQS)


def kernel(
    hid, grad, q_in, q_out, seq, out,
    h_buf, g_buf, own_a, own_b, ring_a, ring_b, part, got, last, landed,
    loc_sem, sib_send, sib_recv, z_send, z_recv, a_send, a_recv, f_send, f_recv,
):
    z, m = lax.axis_index("dp"), lax.axis_index("mp")
    core = lax.rem(m, 2)
    chip = m // 2
    y, x = chip // SIDE, lax.rem(chip, SIDE)
    sibling = (z, chip * 2 + 1 - core)
    along = ((lax.rem(z + 1, NZ), m), (lax.rem(z + NZ - 1, NZ), m))

    mine = pl.ds(core * QH, QH)
    local = [
        pltpu.make_async_copy(src, dst, loc_sem.at[i])
        for i, (src, dst) in enumerate((
            (q_in.at[mine], own_a.at[0]),
            (q_out.at[mine], own_b.at[0]),
            (hid, h_buf.at[0]),
            (grad, g_buf.at[0]),
        ))
    ]
    for copy in local:
        copy.start()

    ready = pltpu.get_barrier_semaphore()
    for target in along:
        pl.semaphore_signal(ready, inc=1, device_id=target, device_id_type=MESH)

    def greet(k, carry):
        pl.semaphore_signal(ready, inc=1, device_id=(z, lax.rem(m + k, 2 * CHIPS)), device_id_type=MESH)
        return carry

    lax.fori_loop(1, 2 * CHIPS, greet, 0)
    pl.semaphore_wait(ready, 2 * CHIPS + 1)

    def to_sibling(i, src, dst):
        return pltpu.make_async_remote_copy(src, dst, sib_send.at[i], sib_recv.at[i], sibling, MESH)

    theirs = pl.ds((1 - core) * QH, QH)
    swap = [
        to_sibling(0, q_in.at[theirs], own_a.at[1]),
        to_sibling(1, q_out.at[theirs], own_b.at[1]),
        to_sibling(2, hid, h_buf.at[1]),
        to_sibling(3, grad, g_buf.at[1]),
    ]

    def hop(d, s, j):
        if s > 0:
            a, b = ring_a.at[d, s - 1, j], ring_b.at[d, s - 1, j]
        elif j == 0:
            a, b = q_in.at[mine], q_out.at[mine]
        else:
            a, b = own_a.at[1], own_b.at[1]
        return [
            pltpu.make_async_remote_copy(
                src, dst.at[d, s, j], z_send.at[d, s, j, i], z_recv.at[d, s, j, i], along[d], MESH
            )
            for i, (src, dst) in enumerate(((a, ring_a), (b, ring_b)))
        ]

    hops = {(d, s, j): hop(d, s, j) for s in range(4) for j in range(2) for d in range(2) if s < 3 or d == j}

    def start(copies):
        for copy in copies:
            copy.start()

    def arrived(copies):
        for copy in copies:
            copy.wait_recv()

    start(swap[:2])
    for d in range(2):
        start(hops[d, 0, 0])
    start(swap[2:])
    arrived(swap[:2])
    for d in range(2):
        start(hops[d, 0, 1])

    def project(p, halves):
        for at, blocks, tokens in ((0, 0, h_buf), (8, 1, g_buf)):
            total = None
            for j, half in enumerate(halves):
                rows = half[blocks][...].reshape(QH * R, tokens.shape[2])
                term = lax.dot_general(rows, tokens[j], NT, preferred_element_type=jnp.float32)
                total = term if total is None else total + term
            part[p, :, at : at + 8, :] = total.reshape(CHIPS, 8, TOK)

    def peer(k):
        return lax.rem(y + k // SIDE, SIDE) * SIDE + lax.rem(x + lax.rem(k, SIDE), SIDE)

    def spread(p):
        def send(k, carry):
            target = peer(k)
            pltpu.make_async_remote_copy(
                part.at[p, target], got.at[p, k - 1], a_send.at[p], a_recv.at[p], (z, target * 2 + core), MESH
            ).start()
            return carry

        lax.fori_loop(1, CHIPS, send, 0)

    label = lax.broadcasted_iota(jnp.int32, (SEQS, TOK), 0)
    member = seq[...] == label

    def add_up(p):
        pltpu.make_async_copy(got.at[p], got.at[p], a_recv.at[p]).wait()
        total = part[p, chip]
        for k in range(CHIPS - 1):
            total = total + got[p, k]
        score = jnp.sum(total[:8] * total[8:], axis=0, keepdims=True)
        by_seq = jnp.where(member, score, 0.0)
        lanes = by_seq[:, :128]
        for t in range(1, TOK // 128):
            lanes = lanes + by_seq[:, t * 128 : (t + 1) * 128]
        last[p] = lanes

    def final_copy(p, step):
        origin = lax.rem(z + step + NZ, NZ)
        owner = (2 * origin + core) * 2 + chip // 8
        slot = lax.rem(chip, 8)
        away = pltpu.make_async_remote_copy(
            last.at[p], landed.at[slot], f_send.at[p], f_recv.at[0], (z, owner), MESH
        )
        here = pltpu.make_async_copy(last.at[p], landed.at[slot], f_recv.at[0])
        return owner == m, away, here

    steps = [0, -1, 1, -2, 2, -3, 3, 4]

    def finish(p):
        add_up(p)
        own, away, here = final_copy(p, steps[p])
        pl.when(own)(here.start)
        pl.when(jnp.logical_not(own))(away.start)

    for copy in local:
        copy.wait()
    arrived(swap[2:])
    project(0, [(own_a.at[0], own_b.at[0]), (own_a.at[1], own_b.at[1])])
    spread(0)
    for s in range(3):
        for j in range(2):
            for d in range(2):
                arrived(hops[d, s, j])
                if (d, s + 1, j) in hops:
                    start(hops[d, s + 1, j])
        for d in range(2):
            p = 1 + 2 * s + d
            project(p, [(ring_a.at[d, s, j], ring_b.at[d, s, j]) for j in range(2)])
            spread(p)
        for p in ([0] if s == 0 else [2 * s - 1, 2 * s]):
            finish(p)
    for d in range(2):
        arrived(hops[d, 3, d])
    project(7, [(ring_a.at[j, 3, j], ring_b.at[j, 3, j]) for j in range(2)])
    spread(7)
    for p in (5, 6, 7):
        finish(p)

    for copy in swap:
        copy.wait_send()
    for copies in hops.values():
        for copy in copies:
            copy.wait_send()
    for p in range(NZ):
        pltpu.make_async_copy(got.at[p], got.at[p], a_send.at[p]).wait()
        own, away, here = final_copy(p, steps[p])
        pl.when(jnp.logical_not(own))(away.wait_send)

    pltpu.make_async_copy(landed, landed, f_recv.at[0]).wait()
    for q in range(2):
        total = (landed[4 * q] + landed[4 * q + 1]) + (landed[4 * q + 2] + landed[4 * q + 3])
        out[:, q : q + 1] = jnp.sum(total, axis=1, keepdims=True) * SCALE


def body(hidden_acts, out_grads, query_in, query_out, seq_ids):
    ff, width = hidden_acts.shape[1], out_grads.shape[1]
    any_spec = pl.BlockSpec(memory_space=pl.ANY)
    vmem_spec = pl.BlockSpec(memory_space=pltpu.VMEM)
    dma = pltpu.SemaphoreType.DMA
    bf16, f32 = jnp.bfloat16, jnp.float32
    return pl.pallas_call(
        kernel,
        out_shape=jax.ShapeDtypeStruct((SEQS, 2), f32),
        in_specs=[any_spec] * 4 + [vmem_spec],
        out_specs=vmem_spec,
        scratch_shapes=[
            pltpu.VMEM((2, TOK, ff), bf16),
            pltpu.VMEM((2, TOK, width), bf16),
            pltpu.VMEM((2, QH, R, ff), bf16),
            pltpu.VMEM((2, QH, R, width), bf16),
            pltpu.VMEM((2, 4, 2, QH, R, ff), bf16),
            pltpu.VMEM((2, 4, 2, QH, R, width), bf16),
            pltpu.VMEM((NZ, CHIPS, 16, TOK), f32),
            pltpu.VMEM((NZ, CHIPS - 1, 16, TOK), f32),
            pltpu.VMEM((NZ, SEQS, 128), f32),
            pltpu.VMEM((8, SEQS, 128), f32),
            dma((4,)),
            dma((4,)),
            dma((4,)),
            dma((2, 4, 2, 2)),
            dma((2, 4, 2, 2)),
            dma((NZ,)),
            dma((NZ,)),
            dma((NZ,)),
            dma((1,)),
        ],
        compiler_params=pltpu.CompilerParams(
            collective_id=0, has_side_effects=True, vmem_limit_bytes=48 * 2**20
        ),
    )(hidden_acts, out_grads, query_in, query_out, seq_ids)


def solution(mesh):
    placed = (P("dp", "mp"), P("dp", "mp"), P("dp", None, "mp"), P("dp", None, "mp"), P("dp", None))
    return jax.shard_map(body, mesh=mesh, in_specs=placed, out_specs=P("dp", "mp"), check_vma=False)
```

time: 224 us -> 89.7 us (0.40)
  waiting for transfers between devices: 192 us -> 0 us
  Pallas kernels: 0 us -> 84 us
  between operations: 13.1 us -> 0.01 us
  matrix products: 10.8 us -> 0 us
  other arithmetic: 5.7 us -> 0 us
  local copies, waits for them, and re-layouts: 0.67 us -> 5.47 us
    reduce_scatter x1 -> x0, waiting for transfers between devices: 102 us -> none  [body(): lax.psum_scatter(jnp.stack([proj_in, proj_out], axis=1), 'mp', scatter_di...]
    all_gather x2 -> x0, waiting for transfers between devices: 88.2 us -> none  [the longest x1 50.7 us: body(): lax.all_gather(query_in, 'dp', axis=0, tiled=True)]
    pallas_call x0 -> x1, Pallas kernels: none -> 84 us  [body(): pl.pallas_call(kernel, out_shape=jax.ShapeDtypeStruct((SEQS, 2), f32), in...]
    dot_general x3 -> x0, matrix products: 10.8 us -> none  [the longest x1 5.52 us: body(): lax.dot_general(in_rows, hidden_acts, contract, preferred_element_type=jn...]
    another operation x1 -> x0, other arithmetic: 4.64 us -> none  [body(): jnp.stack([proj_in, proj_out], axis=1)]
    unnamed x6 -> x10, local copies, waits for them, and re-layouts: 0.67 us -> 4.83 us
  transfers between devices with their start and end apart: 3 -> 0, of which waited for: 3 -> 0; matrix products, arithmetic and copies ran while one was open for 2% -> 0% of each run, Pallas kernels for 0% -> 0%
where the time goes in v1:
time: 89.7 us; the launch traced here: 89.5 us
  Pallas kernels  84 us (94%)
  local copies, waits for them, and re-layouts  5.47 us (6%)
    pallas_call x1, Pallas kernels, body(): pl.pallas_call(kernel, out_shape=jax.ShapeDtypeStruct((SEQS, 2), f32), in...  84 us
    unnamed x10, local copies, waits for them, and re-layouts  4.83 us

profile of v1, /device:TPU:17, one launch (start us, length us, event | category | flops | bytes accessed | tf_op | source)
XLA Modules:
  0.0 89.5 jit_solution(17091918109691872872)
XLA Ops:
  0.0 0.0 copy-start
  0.0 1.3 %copy-done = bf16[640,896]{1,0:T(8,128)(2,1)S(1)} copy-done((bf16[640,896]{1,0:T(8,128)(2,1)S(1)}, bf16[640,896]{1,0:T(8,128)(2,1)}, u32[]{:S(2)}) %copy-start) | copy-done | bytes 1146904
  1.3 0.0 copy-start.1
  1.3 1.0 %copy-done.1 = bf16[8,32,896]{2,1,0:T(8,128)(2,1)S(1)} copy-done((bf16[8,32,896]{2,1,0:T(8,128)(2,1)S(1)}, bf16[8,32,896]{2,1,0:T(8,128)(2,1)}, u32[]{:S(2)}) %copy-start.1) | copy-done | bytes 458776
  2.3 0.0 copy-start.2
  2.3 1.0 %copy-done.2 = bf16[640,256]{1,0:T(8,128)(2,1)S(1)} copy-done((bf16[640,256]{1,0:T(8,128)(2,1)S(1)}, bf16[640,256]{1,0:T(8,128)(2,1)}, u32[]{:S(2)}) %copy-start.2) | copy-done | bytes 327704
  3.3 0.0 copy-start.3
  3.3 0.9 %copy-done.3 = bf16[8,32,256]{2,1,0:T(8,128)(2,1)S(1)} copy-done((bf16[8,32,256]{2,1,0:T(8,128)(2,1)S(1)}, bf16[8,32,256]{2,1,0:T(8,128)(2,1)}, u32[]{:S(2)}) %copy-start.3) | copy-done | bytes 131096
  4.2 0.0 copy-start.4
  4.2 0.7 copy-done.4
  4.8 84.0 %shard_map.55 = f32[16,2]{1,0:T(8,128)S(1)} custom-call(bf16[640,896]{1,0:T(8,128)(2,1)S(1)} %copy-done, bf16[640,256]{1,0:T(8,128)(2,1)S(1)} %copy-done.2, bf16[8,32,896]{2,1,0:T(8,128)(2,1)S(1)} %copy-done.1, bf16[8,32,256]{2,1,0:T(8,128)(2,1)S(1)} %copy-done.3, s32[1,640]{1,0:T(1,128)S(1)} %copy-done.4), custom_call_target="tpu_custom_call" | custom-call | tf_op jit(solution)/shard_map/pallas_call | solution.py:203
  88.9 0.6 copy.6
Async XLA Ops:
  0.0 1.3 %copy-start = (bf16[640,896]{1,0:T(8,128)(2,1)S(1)}, bf16[640,896]{1,0:T(8,128)(2,1)}, u32[]{:S(2)}) copy-start(bf16[640,896]{1,0:T(8,128)(2,1)} %hid.1) | copy-start | bytes 3440644
  1.3 1.0 %copy-start.1 = (bf16[8,32,896]{2,1,0:T(8,128)(2,1)S(1)}, bf16[8,32,896]{2,1,0:T(8,128)(2,1)}, u32[]{:S(2)}) copy-start(bf16[8,32,896]{2,1,0:T(8,128)(2,1)} %q_in.1) | copy-start | bytes 1376260
  2.3 1.0 %copy-start.2 = (bf16[640,256]{1,0:T(8,128)(2,1)S(1)}, bf16[640,256]{1,0:T(8,128)(2,1)}, u32[]{:S(2)}) copy-start(bf16[640,256]{1,0:T(8,128)(2,1)} %grad.1) | copy-start | bytes 983044
  3.3 0.9 %copy-start.3 = (bf16[8,32,256]{2,1,0:T(8,128)(2,1)S(1)}, bf16[8,32,256]{2,1,0:T(8,128)(2,1)}, u32[]{:S(2)}) copy-start(bf16[8,32,256]{2,1,0:T(8,128)(2,1)} %q_out.1) | copy-start | bytes 393220
  4.2 0.7 copy-start.4

commit v2 on v1

--- a/solution.py
+++ b/solution.py
@@ -17,12 +17,14 @@
 QH = 4
 MESH = pl.DeviceIdType.MESH
 NT = (((1,), (1,)), ((), ()))
+TILES = TOK // 128
+WIDE = TOK + 128
 SCALE = 1.0 / math.sqrt(R * TOK / SEQS)
 
 
 def kernel(
     hid, grad, q_in, q_out, seq, out,
-    h_buf, g_buf, own_a, own_b, ring_a, ring_b, part, got, last, landed,
+    h_buf, g_buf, own_a, own_b, ring_a, ring_b, ids, proj, part, got, last, landed,
     loc_sem, sib_send, sib_recv, z_send, z_recv, a_send, a_recv, f_send, f_recv,
 ):
     z, m = lax.axis_index("dp"), lax.axis_index("mp")
@@ -40,6 +42,7 @@
             (q_out.at[mine], own_b.at[0]),
             (hid, h_buf.at[0]),
             (grad, g_buf.at[0]),
+            (seq, ids),
         ))
     ]
     for copy in local:
@@ -100,13 +103,32 @@
         start(hops[d, 0, 1])
 
     def project(p, halves):
-        for at, blocks, tokens in ((0, 0, h_buf), (8, 1, g_buf)):
+        for which, tokens in enumerate((h_buf, g_buf)):
             total = None
             for j, half in enumerate(halves):
-                rows = half[blocks][...].reshape(QH * R, tokens.shape[2])
+                rows = half[which][...].reshape(QH * R, tokens.shape[2])
                 term = lax.dot_general(rows, tokens[j], NT, preferred_element_type=jnp.float32)
                 total = term if total is None else total + term
-            part[p, :, at : at + 8, :] = total.reshape(CHIPS, 8, TOK)
+            proj[which] = total.reshape(CHIPS, 8, TOK)
+
+        row = lax.broadcasted_iota(jnp.int32, (8, 128), 0)
+
+        def pack(i, carry):
+            for t in range(TILES):
+                at = slice(t * 128, (t + 1) * 128)
+                coded = []
+                for which in range(2):
+                    value = proj[which, i, :, at]
+                    top = jnp.max(jnp.abs(value), axis=0, keepdims=True)
+                    power = jnp.ceil(jnp.log2(jnp.maximum(top, 2.0**-100) * 1.0001)) - 15.0
+                    coded.append(jnp.round(value * jnp.exp2(-power)))
+                    carry = carry[:which] + (jnp.where(row == t, power, carry[which]),) + carry[which + 1 :]
+                part[p, i, :, at] = jnp.concatenate(coded, axis=0).astype(jnp.int32).astype(jnp.int16)
+            part[p, i, :, TOK:] = jnp.concatenate(carry, axis=0).astype(jnp.int32).astype(jnp.int16)
+            return carry
+
+        none = jnp.zeros((8, 128), jnp.float32)
+        lax.fori_loop(0, CHIPS, pack, (none, none))
 
     def peer(k):
         return lax.rem(y + k // SIDE, SIDE) * SIDE + lax.rem(x + lax.rem(k, SIDE), SIDE)
@@ -121,19 +143,26 @@
 
         lax.fori_loop(1, CHIPS, send, 0)
 
-    label = lax.broadcasted_iota(jnp.int32, (SEQS, TOK), 0)
-    member = seq[...] == label
+    label = lax.broadcasted_iota(jnp.int32, (SEQS, 128), 0)
 
     def add_up(p):
         pltpu.make_async_copy(got.at[p], got.at[p], a_recv.at[p]).wait()
-        total = part[p, chip]
-        for k in range(CHIPS - 1):
-            total = total + got[p, k]
-        score = jnp.sum(total[:8] * total[8:], axis=0, keepdims=True)
-        by_seq = jnp.where(member, score, 0.0)
-        lanes = by_seq[:, :128]
-        for t in range(1, TOK // 128):
-            lanes = lanes + by_seq[:, t * 128 : (t + 1) * 128]
+        lanes = jnp.zeros((SEQS, 128), jnp.float32)
+        powers = []
+        for k in range(CHIPS):
+            message = part.at[p, chip] if k == 0 else got.at[p, k - 1]
+            powers.append(jnp.exp2(message[:, TOK:].astype(jnp.int32).astype(jnp.float32)))
+        for t in range(TILES):
+            at = slice(t * 128, (t + 1) * 128)
+            total = [jnp.zeros((8, 128), jnp.float32)] * 2
+            for k in range(CHIPS):
+                message = part.at[p, chip] if k == 0 else got.at[p, k - 1]
+                value = message[:, at].astype(jnp.int32).astype(jnp.float32)
+                for which in range(2):
+                    power = powers[k][which * 8 + t : which * 8 + t + 1]
+                    total[which] = total[which] + value[which * 8 : which * 8 + 8] * power
+            score = jnp.sum(total[0] * total[1], axis=0, keepdims=True)
+            lanes = lanes + jnp.where(ids[:, at] == label, score, 0.0)
         last[p] = lanes
 
     def final_copy(p, step):
@@ -196,14 +225,14 @@
 
 def body(hidden_acts, out_grads, query_in, query_out, seq_ids):
     ff, width = hidden_acts.shape[1], out_grads.shape[1]
-    any_spec = pl.BlockSpec(memory_space=pl.ANY)
+    hbm_spec = pl.BlockSpec(memory_space=pltpu.MemorySpace.HBM)
     vmem_spec = pl.BlockSpec(memory_space=pltpu.VMEM)
     dma = pltpu.SemaphoreType.DMA
     bf16, f32 = jnp.bfloat16, jnp.float32
     return pl.pallas_call(
         kernel,
         out_shape=jax.ShapeDtypeStruct((SEQS, 2), f32),
-        in_specs=[any_spec] * 4 + [vmem_spec],
+        in_specs=[hbm_spec] * 5,
         out_specs=vmem_spec,
         scratch_shapes=[
             pltpu.VMEM((2, TOK, ff), bf16),
@@ -212,11 +241,13 @@
             pltpu.VMEM((2, QH, R, width), bf16),
             pltpu.VMEM((2, 4, 2, QH, R, ff), bf16),
             pltpu.VMEM((2, 4, 2, QH, R, width), bf16),
-            pltpu.VMEM((NZ, CHIPS, 16, TOK), f32),
-            pltpu.VMEM((NZ, CHIPS - 1, 16, TOK), f32),
+            pltpu.VMEM((1, TOK), jnp.int32),
+            pltpu.VMEM((2, CHIPS, 8, TOK), f32),
+            pltpu.VMEM((NZ, CHIPS, 16, WIDE), jnp.int16),
+            pltpu.VMEM((NZ, CHIPS - 1, 16, WIDE), jnp.int16),
             pltpu.VMEM((NZ, SEQS, 128), f32),
             pltpu.VMEM((8, SEQS, 128), f32),
-            dma((4,)),
+            dma((5,)),
             dma((4,)),
             dma((4,)),
             dma((2, 4, 2, 2)),
@@ -227,7 +258,7 @@
             dma((1,)),
         ],
         compiler_params=pltpu.CompilerParams(
-            collective_id=0, has_side_effects=True, vmem_limit_bytes=48 * 2**20
+            collective_id=0, has_side_effects=True, vmem_limit_bytes=63 * 2**20
         ),
     )(hidden_acts, out_grads, query_in, query_out, seq_ids)
 

time: 89.7 us -> 74.6 us (0.83)
  Pallas kernels: 84 us -> 73.1 us
  local copies, waits for them, and re-layouts: 5.47 us -> 1.33 us
    pallas_call x1, Pallas kernels: 84 us -> 73.1 us  [body(): pl.pallas_call(kernel, out_shape=jax.ShapeDtypeStruct((SEQS, 2), f32), in...]
    unnamed x10 -> x0, local copies, waits for them, and re-layouts: 4.83 us -> none
where the time goes in v2:
time: 74.6 us; the launch traced here: 74.5 us
  Pallas kernels  73.1 us (98%)
  local copies, waits for them, and re-layouts  1.33 us (2%)
    pallas_call x1, Pallas kernels, body(): pl.pallas_call(kernel, out_shape=jax.ShapeDtypeStruct((SEQS, 2), f32), in...  73.1 us

profile of v2, /device:TPU:17, one launch (start us, length us, event | category | flops | bytes accessed | tf_op | source)
XLA Modules:
  0.0 74.5 jit_solution(9493960561281107356)
XLA Ops:
  0.0 73.1 %shard_map.55 = f32[16,2]{1,0:T(8,128)} custom-call(bf16[640,896]{1,0:T(8,128)(2,1)} %hid.1, bf16[640,256]{1,0:T(8,128)(2,1)} %grad.1, bf16[8,32,896]{2,1,0:T(8,128)(2,1)} %q_in.1, bf16[8,32,256]{2,1,0:T(8,128)(2,1)} %q_out.1, s32[1,640]{1,0:T(1,128)} %seq.1), custom_call_target="tpu_custom_call" | custom-call | tf_op jit(solution)/shard_map/pallas_call | solution.py:232
  73.1 1.3 %copy.6 = f32[16,2]{0,1:T(2,128)} copy(f32[16,2]{1,0:T(8,128)} %shard_map.55) | data formatting | bytes 256 | tf_op jit(solution)/shard_map/pallas_call | solution.py:232

commit v3 on v2

v3 whole, which is shorter than its diff:
```python
import functools
import math

import jax
import jax.numpy as jnp
from jax import lax
from jax.experimental import pallas as pl
from jax.experimental.pallas import tpu as pltpu
from jax.sharding import PartitionSpec as P

R = 32
TOK = 640
SEQS = 16
NZ = 8
SIDE = 4
CHIPS = SIDE * SIDE
QH = 4
QC = 2
MESH = pl.DeviceIdType.MESH
NT = (((1,), (1,)), ((), ()))
TILES = TOK // 128
WIDE = TOK + 128
SCALE = 1.0 / math.sqrt(R * TOK / SEQS)


def kernel(
    hid, grad, q_in, q_out, seq, out,
    h_buf, g_buf, own, ring, ids, proj, part, got, last, landed,
    loc_sem, sib_send, sib_recv, z_send, z_recv, a_send, a_recv, f_send, f_recv, known,
):
    z, m = lax.axis_index("dp"), lax.axis_index("mp")
    core = lax.rem(m, 2)
    chip = m // 2
    y, x = chip // SIDE, lax.rem(chip, SIDE)

    def at(row, column):
        return (z, (lax.rem(row + SIDE, SIDE) * SIDE + lax.rem(column + SIDE, SIDE)) * 2 + core)

    sibling = (z, chip * 2 + 1 - core)
    along = ((lax.rem(z + 1, NZ), m), (lax.rem(z + NZ - 1, NZ), m))
    beside_x = (at(y, x + 1), at(y, x - 1))
    beside_y = (at(y + 1, x), at(y - 1, x))

    ff = hid.shape[1]

    def queries(of_core, half):
        return pl.ds(of_core * QH + half * QC, QC)

    local = [
        pltpu.make_async_copy(src, dst, loc_sem.at[i])
        for i, (src, dst) in enumerate((
            (q_in.at[queries(core, 0)], own.at[0, 0, :, :, :ff]),
            (q_out.at[queries(core, 0)], own.at[0, 0, :, :, ff:]),
            (q_in.at[queries(core, 1)], own.at[0, 1, :, :, :ff]),
            (q_out.at[queries(core, 1)], own.at[0, 1, :, :, ff:]),
            (hid, h_buf.at[0]),
            (grad, g_buf.at[0]),
            (seq, ids),
        ))
    ]
    for copy in local:
        copy.start()

    ready = pltpu.get_barrier_semaphore()
    for target in (*along, sibling, *beside_x, *beside_y):
        pl.semaphore_signal(ready, inc=1, device_id=target, device_id_type=MESH)
    pl.semaphore_wait(ready, 7)

    swap = [
        pltpu.make_async_remote_copy(src, dst, sib_send.at[i], sib_recv.at[i], sibling, MESH)
        for i, (src, dst) in enumerate((
            (q_in.at[queries(1 - core, 0)], own.at[1, 0, :, :, :ff]),
            (q_out.at[queries(1 - core, 0)], own.at[1, 0, :, :, ff:]),
            (q_in.at[queries(1 - core, 1)], own.at[1, 1, :, :, :ff]),
            (q_out.at[queries(1 - core, 1)], own.at[1, 1, :, :, ff:]),
            (hid, h_buf.at[1]),
            (grad, g_buf.at[1]),
        ))
    ]

    def hop(d, s, h, j):
        src = own.at[j, h] if s == 0 else ring.at[s - 1, h, j, d]
        dst = ring.at[s, h if s < 3 else 0, j, d]
        return pltpu.make_async_remote_copy(
            src, dst, z_send.at[s, h, j, d], z_recv.at[s, h, j, d], along[d], MESH
        )

    hops = {
        (d, s, h, j): hop(d, s, h, j)
        for s in range(4) for h in range(2) for j in range(2) for d in range(2) if s < 3 or d == h
    }

    for copy in swap[:2]:
        copy.start()
    for copy in local[:4]:
        copy.wait()
    for d in range(2):
        hops[d, 0, 0, 0].start()
    for copy in swap[2:]:
        copy.start()
    for h in range(2):
        if h == 1:
            for d in range(2):
                hops[d, 0, 1, 0].start()
        for copy in swap[2 * h : 2 * h + 2]:
            copy.wait_recv()
        for d in range(2):
            hops[d, 0, h, 1].start()

    for i, targets in enumerate((beside_x, beside_y, beside_y, (sibling,))):
        for target in targets:
            pl.semaphore_signal(known.at[i], inc=1, device_id=target, device_id_type=MESH)
        pl.semaphore_wait(known.at[i], len(targets))

    row = lax.broadcasted_iota(jnp.int32, (8, 128), 0)

    def project(p, feature_halves):
        for which, (tokens, columns) in enumerate(((h_buf, slice(0, ff)), (g_buf, slice(ff, None)))):
            total = None
            for j, half in enumerate(feature_halves):
                rows = half[:, :, :, columns].reshape(QH * R, tokens.shape[2])
                term = lax.dot_general(rows, tokens[j], NT, preferred_element_type=jnp.float32)
                total = term if total is None else total + term
            proj[which] = total.reshape(CHIPS, 8, TOK)

        def pack(i, carry):
            for t in range(TILES):
                at = slice(t * 128, (t + 1) * 128)
                coded = []
                for which in range(2):
                    value = proj[which, i, :, at]
                    top = jnp.max(jnp.abs(value), axis=0, keepdims=True)
                    power = jnp.ceil(jnp.log2(jnp.maximum(top, 2.0**-100) * 1.0001)) - 15.0
                    coded.append(jnp.round(value * jnp.exp2(-power)))
                    carry = carry[:which] + (jnp.where(row == t, power, carry[which]),) + carry[which + 1 :]
                part[p, i, :, at] = jnp.concatenate(coded, axis=0).astype(jnp.int32).astype(jnp.int16)
            part[p, i, :, TOK:] = jnp.concatenate(carry, axis=0).astype(jnp.int32).astype(jnp.int16)
            return carry

        none = jnp.zeros((8, 128), jnp.float32)
        lax.fori_loop(0, CHIPS, pack, (none, none))

    def spread(p):
        def send(k, carry):
            target = lax.rem(y + k // SIDE, SIDE) * SIDE + lax.rem(x + lax.rem(k, SIDE), SIDE)
            pltpu.make_async_remote_copy(
                part.at[p, target], got.at[p, k - 1], a_send.at[p], a_recv.at[p], (z, target * 2 + core), MESH
            ).start()
            return carry

        lax.fori_loop(1, CHIPS, send, 0)

    label = lax.broadcasted_iota(jnp.int32, (SEQS, 128), 0)

    def add_up(p):
        pltpu.make_async_copy(got.at[p], got.at[p], a_recv.at[p]).wait()
        lanes = jnp.zeros((SEQS, 128), jnp.float32)
        powers = []
        for k in range(CHIPS):
            message = part.at[p, chip] if k == 0 else got.at[p, k - 1]
            powers.append(jnp.exp2(message[:, TOK:].astype(jnp.int32).astype(jnp.float32)))
        for t in range(TILES):
            at = slice(t * 128, (t + 1) * 128)
            total = [jnp.zeros((8, 128), jnp.float32)] * 2
            for k in range(CHIPS):
                message = part.at[p, chip] if k == 0 else got.at[p, k - 1]
                value = message[:, at].astype(jnp.int32).astype(jnp.float32)
                for which in range(2):
                    power = powers[k][which * 8 + t : which * 8 + t + 1]
                    total[which] = total[which] + value[which * 8 : which * 8 + 8] * power
            score = jnp.sum(total[0] * total[1], axis=0, keepdims=True)
            lanes = lanes + jnp.where(ids[:, at] == label, score, 0.0)
        last[p] = lanes

    upper = chip // 8

    def final_copy(p):
        if p in (0, 7):
            origin, half = z + (0 if p == 0 else 4), upper
        else:
            s, half = divmod(p - 1, 2)
            origin = z + NZ + (2 * upper - 1) * (s + 1)
        owner = (2 * lax.rem(origin, NZ) + core) * 2 + half
        slot = lax.rem(chip, 8)
        away = pltpu.make_async_remote_copy(
            last.at[p], landed.at[slot], f_send.at[p], f_recv.at[0], (z, owner), MESH
        )
        here = pltpu.make_async_copy(last.at[p], landed.at[slot], f_recv.at[0])
        return owner == m, away, here

    def finish(p):
        add_up(p)
        mine, away, here = final_copy(p)
        pl.when(mine)(here.start)
        pl.when(jnp.logical_not(mine))(away.start)

    for copy in local[4:]:
        copy.wait()
    for copy in swap[4:]:
        copy.wait_recv()
    project(0, [own.at[j] for j in range(2)])
    spread(0)
    for s in range(4):
        for h in range(2 if s < 3 else 1):
            for j in range(2):
                for d in range(2):
                    stop = (d, s, h if s < 3 else d, j)
                    hops[stop].wait_recv()
                    onward = (d, s + 1, h, j)
                    if onward in hops:
                        hops[onward].start()
            p = 1 + 2 * s + h
            project(p, [ring.at[s, h, j] for j in range(2)])
            spread(p)
            finish(p - 1)
    finish(7)

    for copy in swap:
        copy.wait_send()
    for copy in hops.values():
        copy.wait_send()
    for p in range(NZ):
        pltpu.make_async_copy(got.at[p], got.at[p], a_send.at[p]).wait()
        mine, away, here = final_copy(p)
        pl.when(jnp.logical_not(mine))(away.wait_send)

    pltpu.make_async_copy(landed, landed, f_recv.at[0]).wait()
    for q in range(2):
        total = (landed[4 * q] + landed[4 * q + 1]) + (landed[4 * q + 2] + landed[4 * q + 3])
        out[:, q : q + 1] = jnp.sum(total, axis=1, keepdims=True) * SCALE


def body(hidden_acts, out_grads, query_in, query_out, seq_ids):
    ff, width = hidden_acts.shape[1], out_grads.shape[1]
    hbm_spec = pl.BlockSpec(memory_space=pltpu.MemorySpace.HBM)
    vmem_spec = pl.BlockSpec(memory_space=pltpu.VMEM)
    dma = pltpu.SemaphoreType.DMA
    bf16, f32 = jnp.bfloat16, jnp.float32
    return pl.pallas_call(
        kernel,
        out_shape=jax.ShapeDtypeStruct((SEQS, 2), f32),
        in_specs=[hbm_spec] * 5,
        out_specs=vmem_spec,
        scratch_shapes=[
            pltpu.VMEM((2, TOK, ff), bf16),
            pltpu.VMEM((2, TOK, width), bf16),
            pltpu.VMEM((2, 2, QC, R, ff + width), bf16),
            pltpu.VMEM((4, 2, 2, 2, QC, R, ff + width), bf16),
            pltpu.VMEM((1, TOK), jnp.int32),
            pltpu.VMEM((2, CHIPS, 8, TOK), f32),
            pltpu.VMEM((NZ, CHIPS, 16, WIDE), jnp.int16),
            pltpu.VMEM((NZ, CHIPS - 1, 16, WIDE), jnp.int16),
            pltpu.VMEM((NZ, SEQS, 128), f32),
            pltpu.VMEM((8, SEQS, 128), f32),
            dma((7,)),
            dma((6,)),
            dma((6,)),
            dma((4, 2, 2, 2)),
            dma((4, 2, 2, 2)),
            dma((NZ,)),
            dma((NZ,)),
            dma((NZ,)),
            dma((1,)),
            pltpu.SemaphoreType.REGULAR((4,)),
        ],
        compiler_params=pltpu.CompilerParams(
            collective_id=0, has_side_effects=True, vmem_limit_bytes=63 * 2**20
        ),
    )(hidden_acts, out_grads, query_in, query_out, seq_ids)


def solution(mesh):
    placed = (P("dp", "mp"), P("dp", "mp"), P("dp", None, "mp"), P("dp", None, "mp"), P("dp", None))
    return jax.shard_map(body, mesh=mesh, in_specs=placed, out_specs=P("dp", "mp"), check_vma=False)
```

time: 74.6 us -> 69.4 us (0.930)
  Pallas kernels: 73.1 us -> 67.8 us
    pallas_call x1, Pallas kernels: 73.1 us -> 67.8 us  [body(): pl.pallas_call(kernel, out_shape=jax.ShapeDtypeStruct((SEQS, 2), f32), in...]
where the time goes in v3:
time: 69.4 us; the launch traced here: 69.1 us
  Pallas kernels  67.8 us (98%)
  local copies, waits for them, and re-layouts  1.33 us (2%)
    pallas_call x1, Pallas kernels, body(): pl.pallas_call(kernel, out_shape=jax.ShapeDtypeStruct((SEQS, 2), f32), in...  67.8 us

profile of v3, /device:TPU:17, one launch (start us, length us, event | category | flops | bytes accessed | tf_op | source)
XLA Modules:
  0.0 69.1 jit_solution(15116550755173368482)
XLA Ops:
  0.0 67.8 %shard_map.55 = f32[16,2]{1,0:T(8,128)} custom-call(bf16[640,896]{1,0:T(8,128)(2,1)} %hid.1, bf16[640,256]{1,0:T(8,128)(2,1)} %grad.1, bf16[8,32,896]{2,1,0:T(8,128)(2,1)} %q_in.1, bf16[8,32,256]{2,1,0:T(8,128)(2,1)} %q_out.1, s32[1,640]{1,0:T(1,128)} %seq.1), custom_call_target="tpu_custom_call" | custom-call | tf_op jit(solution)/shard_map/pallas_call | solution.py:239
  67.8 1.3 %copy.6 = f32[16,2]{0,1:T(2,128)} copy(f32[16,2]{1,0:T(8,128)} %shard_map.55) | data formatting | bytes 256 | tf_op jit(solution)/shard_map/pallas_call | solution.py:239

commit v4 on v3

--- a/solution.py
+++ b/solution.py
@@ -114,16 +114,22 @@
 
     row = lax.broadcasted_iota(jnp.int32, (8, 128), 0)
 
+    steps_away = sorted(range(1, CHIPS), key=lambda k: -sum(min(i, SIDE - i) for i in divmod(k, SIDE)))
+
     def project(p, feature_halves):
-        for which, (tokens, columns) in enumerate(((h_buf, slice(0, ff)), (g_buf, slice(ff, None)))):
-            total = None
-            for j, half in enumerate(feature_halves):
+        for j, half in enumerate(feature_halves):
+            half = half()
+            for which, (tokens, columns) in enumerate(((h_buf, slice(0, ff)), (g_buf, slice(ff, None)))):
                 rows = half[:, :, :, columns].reshape(QH * R, tokens.shape[2])
                 term = lax.dot_general(rows, tokens[j], NT, preferred_element_type=jnp.float32)
-                total = term if total is None else total + term
-            proj[which] = total.reshape(CHIPS, 8, TOK)
-
-        def pack(i, carry):
+                term = term.reshape(CHIPS, 8, TOK)
+                if j == 0:
+                    proj[which] = term
+                else:
+                    proj[which] += term
+
+        def pack(i):
+            powers = [jnp.zeros((8, 128), jnp.float32)] * 2
             for t in range(TILES):
                 at = slice(t * 128, (t + 1) * 128)
                 coded = []
@@ -132,23 +138,17 @@
                     top = jnp.max(jnp.abs(value), axis=0, keepdims=True)
                     power = jnp.ceil(jnp.log2(jnp.maximum(top, 2.0**-100) * 1.0001)) - 15.0
                     coded.append(jnp.round(value * jnp.exp2(-power)))
-                    carry = carry[:which] + (jnp.where(row == t, power, carry[which]),) + carry[which + 1 :]
+                    powers[which] = jnp.where(row == t, power, powers[which])
                 part[p, i, :, at] = jnp.concatenate(coded, axis=0).astype(jnp.int32).astype(jnp.int16)
-            part[p, i, :, TOK:] = jnp.concatenate(carry, axis=0).astype(jnp.int32).astype(jnp.int16)
-            return carry
-
-        none = jnp.zeros((8, 128), jnp.float32)
-        lax.fori_loop(0, CHIPS, pack, (none, none))
-
-    def spread(p):
-        def send(k, carry):
-            target = lax.rem(y + k // SIDE, SIDE) * SIDE + lax.rem(x + lax.rem(k, SIDE), SIDE)
+            part[p, i, :, TOK:] = jnp.concatenate(powers, axis=0).astype(jnp.int32).astype(jnp.int16)
+
+        for k in steps_away:
+            target = lax.rem(y + k // SIDE, SIDE) * SIDE + lax.rem(x + k % SIDE, SIDE)
+            pack(target)
             pltpu.make_async_remote_copy(
                 part.at[p, target], got.at[p, k - 1], a_send.at[p], a_recv.at[p], (z, target * 2 + core), MESH
             ).start()
-            return carry
-
-        lax.fori_loop(1, CHIPS, send, 0)
+        pack(chip)
 
     label = lax.broadcasted_iota(jnp.int32, (SEQS, 128), 0)
 
@@ -198,20 +198,18 @@
         copy.wait()
     for copy in swap[4:]:
         copy.wait_recv()
-    project(0, [own.at[j] for j in range(2)])
-    spread(0)
+    project(0, [functools.partial(lambda j: own.at[j], j) for j in range(2)])
+    def arrival(s, h, j):
+        for d in range(2):
+            hops[d, s, h if s < 3 else d, j].wait_recv()
+            if (d, s + 1, h, j) in hops:
+                hops[d, s + 1, h, j].start()
+        return ring.at[s, h, j]
+
     for s in range(4):
         for h in range(2 if s < 3 else 1):
-            for j in range(2):
-                for d in range(2):
-                    stop = (d, s, h if s < 3 else d, j)
-                    hops[stop].wait_recv()
-                    onward = (d, s + 1, h, j)
-                    if onward in hops:
-                        hops[onward].start()
             p = 1 + 2 * s + h
-            project(p, [ring.at[s, h, j] for j in range(2)])
-            spread(p)
+            project(p, [functools.partial(arrival, s, h, j) for j in range(2)])
             finish(p - 1)
     finish(7)
 
@@ -238,7 +236,7 @@
     bf16, f32 = jnp.bfloat16, jnp.float32
     return pl.pallas_call(
         kernel,
-        out_shape=jax.ShapeDtypeStruct((SEQS, 2), f32),
+        out_shape=pltpu.VMEM((SEQS, 2), f32),
         in_specs=[hbm_spec] * 5,
         out_specs=vmem_spec,
         scratch_shapes=[

time: 69.4 us -> 66.4 us (0.957)
  Pallas kernels: 67.8 us -> 65.7 us
    pallas_call x1, Pallas kernels: 67.8 us -> 65.7 us  [body(): pl.pallas_call(kernel, out_shape=pltpu.VMEM((SEQS, 2), f32), in_specs=[hb...]
    pallas_call x1, local copies, waits for them, and re-layouts: 1.33 us -> 0.64 us  [body(): pl.pallas_call(kernel, out_shape=pltpu.VMEM((SEQS, 2), f32), in_specs=[hb...]
where the time goes in v4:
time: 66.4 us; the launch traced here: 66.3 us
  Pallas kernels  65.7 us (99%)
    pallas_call x1, Pallas kernels, body(): pl.pallas_call(kernel, out_shape=pltpu.VMEM((SEQS, 2), f32), in_specs=[hb...  65.7 us

profile of v4, /device:TPU:17, one launch (start us, length us, event | category | flops | bytes accessed | tf_op | source)
XLA Modules:
  0.0 66.3 jit_solution(3443693280394956409)
XLA Ops:
  0.0 65.7 %shard_map.55 = f32[16,2]{1,0:T(8,128)S(1)} custom-call(bf16[640,896]{1,0:T(8,128)(2,1)} %hid.1, bf16[640,256]{1,0:T(8,128)(2,1)} %grad.1, bf16[8,32,896]{2,1,0:T(8,128)(2,1)} %q_in.1, bf16[8,32,256]{2,1,0:T(8,128)(2,1)} %q_out.1, s32[1,640]{1,0:T(1,128)} %seq.1), custom_call_target="tpu_custom_call" | custom-call | tf_op jit(solution)/shard_map/pallas_call | solution.py:237
  65.7 0.6 copy.6

commit v5 on v4

--- a/solution.py
+++ b/solution.py
@@ -26,7 +26,7 @@
 def kernel(
     hid, grad, q_in, q_out, seq, out,
     h_buf, g_buf, own, ring, ids, proj, part, got, last, landed,
-    loc_sem, sib_send, sib_recv, z_send, z_recv, a_send, a_recv, f_send, f_recv, known,
+    loc_sem, sib_send, sib_recv, z_send, z_recv, a_send, a_recv, f_send, f_recv, x_send, known,
 ):
     z, m = lax.axis_index("dp"), lax.axis_index("mp")
     core = lax.rem(m, 2)
@@ -38,8 +38,7 @@
 
     sibling = (z, chip * 2 + 1 - core)
     along = ((lax.rem(z + 1, NZ), m), (lax.rem(z + NZ - 1, NZ), m))
-    beside_x = (at(y, x + 1), at(y, x - 1))
-    beside_y = (at(y + 1, x), at(y - 1, x))
+    beside = (at(y + core, x + 1 - core), at(y - core, x - 1 + core))
 
     ff = hid.shape[1]
 
@@ -62,9 +61,9 @@
         copy.start()
 
     ready = pltpu.get_barrier_semaphore()
-    for target in (*along, sibling, *beside_x, *beside_y):
+    for target in (*along, sibling, *beside):
         pl.semaphore_signal(ready, inc=1, device_id=target, device_id_type=MESH)
-    pl.semaphore_wait(ready, 7)
+    pl.semaphore_wait(ready, 5)
 
     swap = [
         pltpu.make_async_remote_copy(src, dst, sib_send.at[i], sib_recv.at[i], sibling, MESH)
@@ -84,6 +83,16 @@
         return pltpu.make_async_remote_copy(
             src, dst, z_send.at[s, h, j, d], z_recv.at[s, h, j, d], along[d], MESH
         )
+
+    def late_part(query):
+        return ring.at[3, 0, 1, 0, query]
+
+    short = pltpu.make_async_remote_copy(
+        ring.at[2, 0, 1, 0, 0], late_part(0), z_send.at[3, 0, 1, 0], z_recv.at[3, 0, 1, 0], along[0], MESH
+    )
+    extra = pltpu.make_async_remote_copy(
+        ring.at[2, 0, 1, 1, 1], late_part(1), x_send.at[0], z_recv.at[3, 0, 1, 0], along[1], MESH
+    )
 
     hops = {
         (d, s, h, j): hop(d, s, h, j)
@@ -107,7 +116,7 @@
         for d in range(2):
             hops[d, 0, h, 1].start()
 
-    for i, targets in enumerate((beside_x, beside_y, beside_y, (sibling,))):
+    for i, targets in enumerate((beside, beside, (sibling,), beside, beside)):
         for target in targets:
             pl.semaphore_signal(known.at[i], inc=1, device_id=target, device_id_type=MESH)
         pl.semaphore_wait(known.at[i], len(targets))
@@ -202,8 +211,14 @@
     def arrival(s, h, j):
         for d in range(2):
             hops[d, s, h if s < 3 else d, j].wait_recv()
-            if (d, s + 1, h, j) in hops:
-                hops[d, s + 1, h, j].start()
+            onward = (d, s + 1, h, j)
+            if onward == (0, 3, 0, 1):
+                pl.when(z == NZ - 1)(short.start)
+                pl.when(z != NZ - 1)(hops[onward].start)
+            elif onward in hops:
+                hops[onward].start()
+            if (d, s, h, j) == (1, 2, 0, 1):
+                pl.when(z == 1)(extra.start)
         return ring.at[s, h, j]
 
     for s in range(4):
@@ -215,8 +230,13 @@
 
     for copy in swap:
         copy.wait_send()
-    for copy in hops.values():
-        copy.wait_send()
+    for onward, copy in hops.items():
+        if onward == (0, 3, 0, 1):
+            pl.when(z == NZ - 1)(short.wait_send)
+            pl.when(z != NZ - 1)(copy.wait_send)
+        else:
+            copy.wait_send()
+    pl.when(z == 1)(extra.wait_send)
     for p in range(NZ):
         pltpu.make_async_copy(got.at[p], got.at[p], a_send.at[p]).wait()
         mine, away, here = final_copy(p)
@@ -259,7 +279,8 @@
             dma((NZ,)),
             dma((NZ,)),
             dma((1,)),
-            pltpu.SemaphoreType.REGULAR((4,)),
+            dma((1,)),
+            pltpu.SemaphoreType.REGULAR((5,)),
         ],
         compiler_params=pltpu.CompilerParams(
             collective_id=0, has_side_effects=True, vmem_limit_bytes=63 * 2**20

time: 66.4 us -> 65 us (0.979)
  Pallas kernels: 65.7 us -> 64.2 us
    pallas_call x1, Pallas kernels: 65.7 us -> 64.2 us  [body(): pl.pallas_call(kernel, out_shape=pltpu.VMEM((SEQS, 2), f32), in_specs=[hb...]
where the time goes in v5:
time: 65 us; the launch traced here: 64.9 us
  Pallas kernels  64.2 us (99%)
    pallas_call x1, Pallas kernels, body(): pl.pallas_call(kernel, out_shape=pltpu.VMEM((SEQS, 2), f32), in_specs=[hb...  64.2 us

profile of v5, /device:TPU:17, one launch (start us, length us, event | category | flops | bytes accessed | tf_op | source)
XLA Modules:
  0.0 64.9 jit_solution(1906786418870670550)
XLA Ops:
  0.0 64.2 %shard_map.55 = f32[16,2]{1,0:T(8,128)S(1)} custom-call(bf16[640,896]{1,0:T(8,128)(2,1)} %hid.1, bf16[640,256]{1,0:T(8,128)(2,1)} %grad.1, bf16[8,32,896]{2,1,0:T(8,128)(2,1)} %q_in.1, bf16[8,32,256]{2,1,0:T(8,128)(2,1)} %q_out.1, s32[1,640]{1,0:T(1,128)} %seq.1), custom_call_target="tpu_custom_call" | custom-call | tf_op jit(solution)/shard_map/pallas_call | solution.py:257
  64.2 0.6 copy.6
